TPU v7x, 256 devices: a whole 4x4x8 slice. The times are simulated.
256 devices in a mesh: vir: 64 (over x_lo, z, y), occ: 4 (over x_hi, core).
Axes of the slice: x: 4 (x_hi: 2, x_lo: 2; x = x_hi * 2 + x_lo), y: 4, z: 8, core: 2. Of those that a mesh axis runs over, the one named last changes fastest.
Arguments:
- cholesky_c: bfloat16 [2560, 1024, 16], P('vir'), may hold values from -0.75 to 0.75
- cholesky_d: bfloat16 [2560, 1024, 16], P('vir'), may hold values from -0.75 to 0.75
- amplitudes: bfloat16 [512, 256], P('occ'), may hold values from -0.375 to 0.375
Outputs:
- residual: bfloat16 [512, 256, 4096], P('occ', 'vir')
All inputs are finite; a program needn't handle non-finite values.
Results may differ from a plain program's by a relative error of at most 0.0049.
Values may be sent and summed in bfloat16 or wider, within the bound.
A program may use at most 192 MiB of HBM per device.

v0:
```python
import jax
import jax.numpy as jnp
from jax import lax
from jax.sharding import PartitionSpec as P

AH = 64
BH = 64


def body(cholesky_c, cholesky_d, amplitudes):
    vir_size = lax.axis_size("vir")
    occ_size = lax.axis_size("occ")
    occ_index = lax.axis_index("occ")
    local_vectors, orbitals, tile_width = cholesky_c.shape
    row_blocks = orbitals // AH
    col_blocks = orbitals // BH
    blocks_vir = row_blocks * col_blocks // vir_size
    blocks_dev = blocks_vir // occ_size
    targets = jnp.arange(vir_size * blocks_dev, dtype=jnp.int32)
    block_ids = targets // blocks_dev * blocks_vir + occ_index * blocks_dev + targets % blocks_dev
    view_c = cholesky_c.reshape(local_vectors, row_blocks, AH * tile_width)
    view_d = cholesky_d.reshape(local_vectors, col_blocks, BH * tile_width)
    send_c = jnp.take(view_c, block_ids // col_blocks, axis=1)
    send_d = jnp.take(view_d, block_ids % col_blocks, axis=1)
    got_c, got_d = (
        lax.all_to_all(send_c, "vir", split_axis=1, concat_axis=0, tiled=True),
        lax.all_to_all(send_d, "vir", split_axis=1, concat_axis=0, tiled=True),
    )
    all_vectors = vir_size * local_vectors
    left_block = got_c.reshape(all_vectors, blocks_dev, AH, tile_width)
    right_block = got_d.reshape(all_vectors, blocks_dev, BH, tile_width)
    summed = jnp.einsum(
        "qmac,qmbd->mabcd", left_block, right_block, preferred_element_type=jnp.float32
    )
    integrals = summed.reshape(blocks_dev, AH * BH, tile_width * tile_width).astype(jnp.bfloat16)
    return jnp.einsum(
        "ix,mpx->imp",
        amplitudes,
        lax.all_gather(integrals, "occ", axis=0, tiled=True),
        preferred_element_type=jnp.float32,
    ).astype(jnp.bfloat16)


def solution(mesh):
    return jax.shard_map(
        body,
        mesh=mesh,
        in_specs=(P("vir", None, None), P("vir", None, None), P("occ", None)),
        out_specs=P("occ", "vir", None),
        check_vma=False,
    )
```

profile of v0, /device:TPU:1, one launch (start us, length us, event | category | flops | bytes accessed | tf_op | source)
XLA Modules:
  0.0 446.1 jit_solution(6551546012592116583)
XLA Ops:
  6.5 0.0 copy-start
  6.6 7.6 %copy.15 = bf16[40,1024,16]{0,2,1:T(8,128)(2,1)} copy(bf16[40,1024,16]{1,2,0:T(8,128)(2,1)} %param.6) | data formatting | bytes 2621440 | tf_op args[1]
  14.1 3.5 copy.16
  17.7 3.2 gather_fusion
  20.9 5.4 %select_bitcast_fusion.1 = bf16[40,64,1024]{2,0,1:T(8,128)(2,1)} fusion(bf16[64,40,1024]{2,1,0:T(8,128)(2,1)} %gather_fusion, pred[64]{0:T(512)(128)(4,1)S(1)} %compare_and_fusion.1), kind=kLoop, calls=%fused_computation.9 | loop fusion | flops 2621440 | bytes 10485824 | tf_op jit(solution)/shard_map/jit(_take)/select_n | solution.py:24
  26.2 0.0 copy-start.1
  26.2 13.9 %all-to-all-start = ((bf16[40,64,1024]{2,0,1:T(8,128)(2,1)}), bf16[40,64,1024]{2,0,1:T(8,128)(2,1)}, u32[]{:S(2)}, u32[]{:S(2)}) async-start(bf16[40,64,1024]{2,0,1:T(8,128)(2,1)} %select_bitcast_fusion.1), calls=%async_computation | async-start | bytes 10485760 | tf_op jit(solution)/shard_map/all_to_all | solution.py:27
  40.2 0.0 copy-done.1
  40.2 5.4 %copy.18 = bf16[40,1024,16]{0,2,1:T(8,128)(2,1)} copy(bf16[40,1024,16]{1,2,0:T(8,128)(2,1)S(1)} %copy-done.1) | data formatting | bytes 2621440 | tf_op args[0]
  45.6 3.5 copy.19
  49.1 3.2 gather_fusion.1
  52.4 5.4 %select_bitcast_fusion = bf16[40,64,1024]{2,0,1:T(8,128)(2,1)} fusion(bf16[64,40,1024]{2,1,0:T(8,128)(2,1)} %gather_fusion.1, pred[64]{0:T(512)(128)(4,1)S(1)} %compare_and_fusion), kind=kLoop, calls=%fused_computation.8 | loop fusion | flops 2621440 | bytes 10485824 | tf_op jit(solution)/shard_map/jit(_take)/select_n | solution.py:23
  57.8 97.9 %all-to-all-done = bf16[40,64,1024]{2,0,1:T(8,128)(2,1)} async-done(((bf16[40,64,1024]{2,0,1:T(8,128)(2,1)}), bf16[40,64,1024]{2,0,1:T(8,128)(2,1)}, u32[]{:S(2)}, u32[]{:S(2)}) %all-to-all-start) | async-done | bytes 5242912 | tf_op jit(solution)/shard_map/all_to_all | solution.py:27
  155.6 8.7 %all-to-all-start.1 = ((bf16[40,64,1024]{2,0,1:T(8,128)(2,1)}), bf16[40,64,1024]{2,0,1:T(8,128)(2,1)}, u32[]{:S(2)}, u32[]{:S(2)}) async-start(bf16[40,64,1024]{2,0,1:T(8,128)(2,1)} %select_bitcast_fusion), calls=%async_computation.1 | async-start | bytes 10485760 | tf_op jit(solution)/shard_map/all_to_all | solution.py:26
  164.4 0.2 all-gather.2.cloned.1.call-start
  164.6 23.3 %copy.17 = bf16[64,40,1,1024]{1,0,3,2:T(8,128)(2,1)} copy(bf16[64,40,1,1024]{3,1,0,2:T(8,128)(2,1)} %bitcast.3) | data formatting | bytes 10485760 | tf_op jit(solution)/shard_map/all_to_all | solution.py:27
  187.9 24.9 %reshape.65 = bf16[2560,64,16,1]{0,2,1,3:T(8,128)(2,1)} reshape(bf16[64,40,1,1024]{1,0,3,2:T(8,128)(2,1)} %copy.17) | data formatting | bytes 10485760 | tf_op jit(solution)/shard_map/reshape.3
  212.8 66.9 %all-to-all-done.1 = bf16[40,64,1024]{2,0,1:T(8,128)(2,1)} async-done(((bf16[40,64,1024]{2,0,1:T(8,128)(2,1)}), bf16[40,64,1024]{2,0,1:T(8,128)(2,1)}, u32[]{:S(2)}, u32[]{:S(2)}) %all-to-all-start.1) | async-done | bytes 5242912 | tf_op jit(solution)/shard_map/all_to_all | solution.py:26
  279.8 23.3 %copy.20 = bf16[64,40,1,1024]{1,0,3,2:T(8,128)(2,1)} copy(bf16[64,40,1,1024]{3,1,0,2:T(8,128)(2,1)} %bitcast.8) | data formatting | bytes 10485760 | tf_op jit(solution)/shard_map/all_to_all | solution.py:26
  303.1 24.9 %reshape.42 = bf16[2560,64,16]{0,2,1:T(8,128)(2,1)} reshape(bf16[64,40,1,1024]{1,0,3,2:T(8,128)(2,1)} %copy.20) | data formatting | bytes 10485760 | tf_op jit(solution)/shard_map/reshape.4
  328.0 15.5 %convert_bitcast_fusion = bf16[1,64,64,16,16]{1,4,3,2,0:T(8,128)(2,1)} fusion(bf16[2560,64,16]{0,2,1:T(8,128)(2,1)} %reshape.42, bf16[2560,64,16,1]{0,2,1,3:T(8,128)(2,1)} %reshape.65), kind=kOutput, calls=%fused_computation.10 | convolution fusion | flops 5369757696 | bytes 12582912 | tf_op jit(solution)/shard_map/qmac,qmbd->mabcd/dot_general | solution.py:32
  343.5 7.1 %copy.22 = bf16[1,64,64,16,16]{2,1,4,3,0:T(8,128)(2,1)} copy(bf16[1,64,64,16,16]{1,4,3,2,0:T(8,128)(2,1)} %convert_bitcast_fusion) | data formatting | bytes 4194304 | tf_op jit(solution)/shard_map/convert_element_type | solution.py:35
  350.6 5.7 %convert_element_type.29 = bf16[1,4096,256]{1,2,0:T(8,128)(2,1)S(1)} reshape(bf16[1,64,64,16,16]{2,1,4,3,0:T(8,128)(2,1)} %copy.22) | data formatting | bytes 4194304 | tf_op jit(solution)/shard_map/convert_element_type | solution.py:35
  356.3 2.5 copy.23
  358.8 0.0 all-gather.2.cloned.1.call-update
  358.8 64.9 %all-gather.2.cloned.1.call-done = bf16[4,4096,256]{2,1,0:T(8,128)(2,1)} async-done(((bf16[1,4096,256]{2,1,0:T(8,128)(2,1)}), bf16[4,4096,256]{2,1,0:T(8,128)(2,1)}) %all-gather.2.cloned.1.call-update) | async-done | bytes 8388624 | tf_op jit(solution)/shard_map/all_gather | solution.py:39
  423.7 0.0 copy-done
  423.7 7.7 %fusion = bf16[128,4,4096]{0,2,1:T(8,128)(2,1)} fusion(bf16[4,4096,256]{2,1,0:T(8,128)(2,1)} %all-gather.2.cloned.1.call-done, bf16[128,256]{1,0:T(8,128)(2,1)S(1)} %copy-done), kind=kOutput, calls=%fused_computation.3 | convolution fusion | flops 1075838976 | bytes 12648448 | tf_op jit(solution)/shard_map/ix,mpx->imp/dot_general | solution.py:36
  431.4 7.8 %copy.24 = bf16[128,4,4096]{2,1,0:T(4,128)(2,1)} copy(bf16[128,4,4096]{0,2,1:T(8,128)(2,1)} %fusion) | data formatting | bytes 8388608 | tf_op jit(solution)/shard_map/convert_element_type | solution.py:41
  (6 shorter events, 0.1 us)
Async XLA Ops:
  6.5 417.2 %copy-start = (bf16[128,256]{1,0:T(8,128)(2,1)S(1)}, bf16[128,256]{1,0:T(8,128)(2,1)}, u32[]{:S(2)}) copy-start(bf16[128,256]{1,0:T(8,128)(2,1)} %param.7) | copy-start | bytes 196612
  26.2 14.0 %copy-start.1 = (bf16[40,1024,16]{1,2,0:T(8,128)(2,1)S(1)}, bf16[40,1024,16]{1,2,0:T(8,128)(2,1)}, u32[]{:S(2)}) copy-start(bf16[40,1024,16]{1,2,0:T(8,128)(2,1)} %param.5) | copy-start | bytes 3932164
  26.2 129.4 %all-to-all-start = ((bf16[40,64,1024]{2,0,1:T(8,128)(2,1)}), bf16[40,64,1024]{2,0,1:T(8,128)(2,1)}, u32[]{:S(2)}, u32[]{:S(2)}) async-start(bf16[40,64,1024]{2,0,1:T(8,128)(2,1)} %select_bitcast_fusion.1), calls=%async_computation | async-start | bytes 10485760 | tf_op jit(solution)/shard_map/all_to_all | solution.py:27
  155.6 124.1 %all-to-all-start.1 = ((bf16[40,64,1024]{2,0,1:T(8,128)(2,1)}), bf16[40,64,1024]{2,0,1:T(8,128)(2,1)}, u32[]{:S(2)}, u32[]{:S(2)}) async-start(bf16[40,64,1024]{2,0,1:T(8,128)(2,1)} %select_bitcast_fusion), calls=%async_computation.1 | async-start | bytes 10485760 | tf_op jit(solution)/shard_map/all_to_all | solution.py:26
  164.4 259.4 %all-gather.2.cloned.1.call-start = ((), (), s32[]{:S(2)}) async-start(), calls=%async_computation.2 | async-start | bytes 10485760 | tf_op jit(solution)/shard_map/all_gather | solution.py:39
Sparse Core Ops, SparseCore 0:
  358.9 64.7 all-gather.1
where the time goes:
time: 448 us; the launch traced here: 446 us
  waiting for transfers between devices  230 us (51%)
  local copies, waits for them, and re-layouts  146 us (33%)
  matrix products  23.2 us (5%)
  starting transfers between devices  22.9 us (5%)
  between operations  13.5 us (3%)
  other arithmetic  10.8 us (2%)
    all_to_all x1, waiting for transfers between devices, body(): lax.all_to_all(send_d, 'vir', split_axis=1, concat_axis=0, tiled=True)  97.9 us
    all_to_all x1, waiting for transfers between devices, body(): lax.all_to_all(send_c, 'vir', split_axis=1, concat_axis=0, tiled=True)  66.9 us
    all_gather x1, waiting for transfers between devices, body(): lax.all_gather(integrals, 'occ', axis=0, tiled=True)  64.9 us
    another operation x2, local copies, waits for them, and re-layouts  49.9 us
    all_to_all x1, local copies, waits for them, and re-layouts, body(): lax.all_to_all(send_d, 'vir', split_axis=1, concat_axis=0, tiled=True)  23.3 us
    all_to_all x1, local copies, waits for them, and re-layouts, body(): lax.all_to_all(send_c, 'vir', split_axis=1, concat_axis=0, tiled=True)  23.3 us
    dot_general x1, matrix products, body(): jnp.einsum('qmac,qmbd->mabcd', left_block, right_block, preferred_element...  15.5 us
    convert_element_type x3, local copies, waits for them, and re-layouts, body(): summed.reshape(blocks_dev, AH * BH, tile_width * tile_width)  15.2 us
  transfers between devices with their start and end apart: 3, of which 3 were waited for; matrix products, arithmetic and copies ran while one was open for 15% of the time, Pallas kernels for 0%

commit v1 on v0

v1 whole, which is shorter than its diff:
```python
import functools

import jax
import jax.numpy as jnp
from jax import lax
from jax.experimental import pallas as pl
from jax.experimental.pallas import tpu as pltpu
from jax.sharding import PartitionSpec as P

MESH = pl.DeviceIdType.MESH
F32 = jnp.float32
BF16 = jnp.bfloat16

NX, NY, NZ, NK = 4, 4, 8, 2
OFFSETS = (0, -1, 1, -2, 2, -3, 3, 4)
FROM_BELOW = ((-1, 0), (-1, 1), (-2, 0), (-2, 1), (-3, 0), (-3, 1), (4, 0))
FROM_ABOVE = ((1, 1), (1, 0), (2, 1), (2, 0), (3, 1), (3, 0), (4, 1))
GROUPS = ((0, 2), (2, 4), (6, 4), (10, 4), (14, 2))


def slot_of(offset, other):
    return 2 * OFFSETS.index(offset) + other


def place():
    v, o = lax.axis_index("vir"), lax.axis_index("occ")
    x = (o // NK) * 2 + v // (NZ * NY)
    return x, v % NY, (v // NY) % NZ, o % NK


def device(x, y, z, k):
    x, y, z, k = (x + NX) % NX, (y + NY) % NY, (z + NZ) % NZ, (k + NK) % NK
    return ((x % 2) * NZ + z) * NY + y, (x // 2) * NK + k


def kernel(
    c_ref, d_ref, amp_ref, out_ref,
    c_slab, c_send, c_raw, d_raw, rows, c_full, d_full, acc, spread, ints, amps, result,
    load_sem, amp_sems, c1_send, c1_recv, c2_send, c2_recv, c3_send, c3_recv, dy_send, dy_recv,
    z_send, z_recv, x_send, x_recv, out_sem, outs_send, outs_recv,
):
    x, y, z, k = place()
    side = 1 - 2 * k
    low = lax.broadcasted_iota(jnp.int32, (16, 128), 1) < 64

    barrier = pltpu.get_barrier_semaphore()
    greeted = []
    for offset in OFFSETS:
        if offset:
            greeted.append(device(x, y, z + offset, k))
        greeted.append(device(x - side, y, z + offset, k))
    greeted.append(device(x + side, y, z, k))
    greeted += [device(x, y + step, z, k) for step in (1, 2, 3)]
    greeted.append(device(x, y, z, k + 1))
    for target in greeted:
        pl.semaphore_signal(barrier, inc=1, device_id=target, device_id_type=MESH)

    load = pltpu.make_async_copy(c_ref.at[k], c_slab, load_sem.at[0])
    load.start()
    own_d = pltpu.make_async_copy(
        d_ref.at[:, :, :, pl.ds(pl.multiple_of(256 * y + 128 * k, 128), 128)], d_raw.at[:, y], load_sem.at[1]
    )
    own_d.start()
    load.wait()

    def pair_up(p, _):
        for m in range(8):
            first = c_slab[2 * p, :, 128 * m : 128 * (m + 1)].astype(F32)
            second = c_slab[2 * p + 1, :, 128 * m : 128 * (m + 1)].astype(F32)
            c_send[2 * m, p] = jnp.where(low, first, pltpu.roll(second, 64, 1)).astype(BF16)
            c_send[2 * m + 1, p] = jnp.where(low, pltpu.roll(first, 64, 1), second).astype(BF16)
        return 0

    lax.fori_loop(0, 10, pair_up, 0)
    amps[k] = amp_ref[...]

    pl.semaphore_wait(barrier, len(greeted))

    dy = []
    for step in (1, 2, 3):
        to = (y + step) % NY
        copy = pltpu.make_async_remote_copy(
            src_ref=d_ref.at[:, :, :, pl.ds(pl.multiple_of(256 * to + 128 * k, 128), 128)],
            dst_ref=d_raw.at[:, y],
            send_sem=dy_send.at[step - 1], recv_sem=dy_recv.at[step - 1],
            device_id=device(x, to, z, k), device_id_type=MESH,
        )
        copy.start()
        dy.append(copy)

    c1 = {}
    for offset in OFFSETS:
        for other in (0, 1):
            slot = slot_of(offset, other)
            to_x = (x + other * side + NX) % NX
            to_z = (z - offset + NZ) % NZ
            piece = c_send.at[(to_x % 2) * NZ + to_z]
            if slot == 0:
                copy = pltpu.make_async_copy(piece, c_raw.at[0, y], load_sem.at[0])
            else:
                copy = pltpu.make_async_remote_copy(
                    src_ref=piece, dst_ref=c_raw.at[slot, y],
                    send_sem=c1_send.at[slot], recv_sem=c1_recv.at[slot],
                    device_id=device(to_x, y, to_z, k), device_id_type=MESH,
                )
            copy.start()
            c1[slot] = copy
    amp_copy = pltpu.make_async_remote_copy(
        src_ref=amps.at[k], dst_ref=amps.at[k], send_sem=amp_sems.at[0], recv_sem=amp_sems.at[1],
        device_id=device(x, y, z, k + 1), device_id_type=MESH,
    )
    amp_copy.start()

    c2 = {}

    def c_forward(group):
        start, count = GROUPS[group]
        for slot in range(start, start + count):
            if slot == 0:
                c1[slot].wait()
            else:
                c1[slot].wait_recv()
        mine = c_raw.at[pl.ds(start, count), y]
        for step in (1, 3, 2):
            copy = pltpu.make_async_remote_copy(
                src_ref=mine, dst_ref=mine,
                send_sem=c2_send.at[group, step - 1], recv_sem=c2_recv.at[group, step - 1],
                device_id=device(x, y + step, z, k), device_id_type=MESH,
            )
            copy.start()
            c2[group, step] = copy

    c3 = {}

    def c_rows(group):
        start, count = GROUPS[group]
        for step in (1, 2, 3):
            c2[group, step].wait_recv()

        def one_slot(slot, _):
            rows[0:640, :] = c_raw[slot].reshape(640, 128).astype(F32)
            lower = lax.broadcasted_iota(jnp.int32, (40, 128), 1) < 64
            for m in range(8):
                first = rows[pl.ds(2 * m, 40, stride=16), :]
                second = rows[pl.ds(2 * m + 1, 40, stride=16), :]
                both = jnp.concatenate(
                    [
                        jnp.where(lower, first, pltpu.roll(second, 64, 1)),
                        jnp.where(lower, pltpu.roll(first, 64, 1), second),
                    ],
                    axis=0,
                )
                c_full[slot, k, :, 128 * m : 128 * (m + 1)] = both.astype(BF16)
            return 0

        lax.fori_loop(start, start + count, one_slot, 0)
        half = c_full.at[pl.ds(start, count), k]
        c3[group] = pltpu.make_async_remote_copy(
            src_ref=half, dst_ref=half, send_sem=c3_send.at[group], recv_sem=c3_recv.at[group],
            device_id=device(x, y, z, k + 1), device_id_type=MESH,
        )
        c3[group].start()

    sent = []

    def x_copy(h, offset, half):
        copy = pltpu.make_async_remote_copy(
            src_ref=d_full.at[h, slot_of(offset, 0), half],
            dst_ref=d_full.at[h, slot_of(offset, 1), half],
            send_sem=x_send.at[h, half, OFFSETS.index(offset)],
            recv_sem=x_recv.at[h, half, OFFSETS.index(offset)],
            device_id=device(x + 1 - 2 * half, y, z, k), device_id_type=MESH,
        )
        return copy

    def x_start(h, offset, half):
        copy = x_copy(h, offset, half)
        copy.start()
        sent.append(copy)

    def z_copy(h, way, i):
        offset, half = (FROM_BELOW, FROM_ABOVE)[way][i]
        before = (offset + 1 if way == 0 else offset - 1) if offset != 4 else (-3 if way == 0 else 3)
        return pltpu.make_async_remote_copy(
            src_ref=d_full.at[h, slot_of(before, 0), half],
            dst_ref=d_full.at[h, slot_of(offset, 0), half],
            send_sem=z_send.at[h, way, i], recv_sem=z_recv.at[h, way, i],
            device_id=device(x, y, z + 1 - 2 * way, k), device_id_type=MESH,
        )

    def z_start(h, way, i):
        copy = z_copy(h, way, i)
        copy.start()
        sent.append(copy)

    def own_start(h):
        for i in (0, 1):
            for way in (0, 1):
                z_start(h, way, i)
        for half in (0, 1):
            x_start(h, 0, half)

    def step(h, i):
        for way in (0, 1):
            z_copy(h, way, i).wait_recv()
            if i + 2 < 7:
                z_start(h, way, i + 2)
            x_start(h, *(FROM_BELOW, FROM_ABOVE)[way][i])

    def await_x(h, group):
        start, count = GROUPS[group]
        for slot in range(start, start + count, 2):
            for half in (0, 1):
                x_copy(h, OFFSETS[slot // 2], half).wait_recv()

    def multiply(h, group):
        start, count = GROUPS[group]
        last = group == len(GROUPS) - 1

        def one_tile(m, _):
            columns = pl.ds(pl.multiple_of(256 * m, 256), 256)
            left = c_full[start : start + count, :, :, columns].reshape(160 * count, 256)
            right = d_full[h, start : start + count].reshape(160 * count, 1024)
            term = lax.dot_general(left, right, (((0,), (0,)), ((), ())), preferred_element_type=F32)
            if group:
                term += acc[columns, :]
            if not last:
                acc[columns, :] = term
            else:
                for c in range(4):
                    for d in range(8):
                        spread[d, pl.ds(4 * m + c, 64, stride=16), :] = term[
                            64 * c : 64 * (c + 1), 128 * d : 128 * (d + 1)
                        ]
            return 0

        lax.fori_loop(0, 4, one_tile, 0)

    def round_off(h):
        def one_pair(pair, _):
            for d in range(8):
                for odd in (0, 1):
                    at = pl.multiple_of(32 * pair + 16 * odd, 16)
                    ints[pair, 16 * (8 * h + d) : 16 * (8 * h + d + 1), 128 * odd : 128 * (odd + 1)] = (
                        spread[d, pl.ds(at, 16), :].astype(BF16)
                    )
            return 0

        lax.fori_loop(0, 32, one_pair, 0)

    c_forward(0)

    own_d.wait()
    for copy in dy:
        copy.wait_recv()

    def d_rows(half, _):
        rows[...] = d_raw[half].reshape(1280, 128).astype(F32)
        for h in range(2):
            for d in range(8):
                both = jnp.concatenate(
                    [rows[pl.ds(16 * odd + 8 * h + d, 40, stride=32), :] for odd in (0, 1)], axis=0
                )
                d_full[h, 0, half, :, 128 * d : 128 * (d + 1)] = both.astype(BF16)
        return 0

    lax.fori_loop(0, 2, d_rows, 0)
    own_start(0)
    c_forward(1)
    step(0, 0)
    c_forward(2)
    c_rows(0)
    step(0, 1)
    c_forward(3)
    c_rows(1)
    step(0, 2)
    c_forward(4)
    c3[0].wait_recv()
    await_x(0, 0)
    multiply(0, 0)
    step(0, 3)
    c_rows(2)
    step(0, 4)
    c3[1].wait_recv()
    await_x(0, 1)
    multiply(0, 1)
    own_start(1)
    step(0, 5)
    c_rows(3)
    step(0, 6)
    c3[2].wait_recv()
    await_x(0, 2)
    multiply(0, 2)
    step(1, 0)
    c_rows(4)
    c3[3].wait_recv()
    await_x(0, 3)
    multiply(0, 3)
    step(1, 1)
    c3[4].wait_recv()
    await_x(0, 4)
    multiply(0, 4)
    step(1, 2)
    round_off(0)
    await_x(1, 0)
    multiply(1, 0)
    step(1, 3)
    await_x(1, 1)
    multiply(1, 1)
    step(1, 4)
    step(1, 5)
    await_x(1, 2)
    multiply(1, 2)
    step(1, 6)
    await_x(1, 3)
    multiply(1, 3)
    amp_copy.wait_recv()
    await_x(1, 4)
    multiply(1, 4)
    round_off(1)

    lower = lax.broadcasted_iota(jnp.int32, (256, 128), 1) < 64
    finals = []
    for part in range(4):

        def one_pair(pair, _):
            total = jnp.dot(amps[...].reshape(256, 256), ints[pair], preferred_element_type=F32)
            first, second = total[:, :128], total[:, 128:]
            columns = pl.ds(pl.multiple_of(128 * pair, 128), 128)
            result[0, :, columns] = jnp.where(lower, first, pltpu.roll(second, 64, 1)).astype(BF16)
            result[1, :, columns] = jnp.where(lower, pltpu.roll(first, 64, 1), second).astype(BF16)
            return 0

        lax.fori_loop(8 * part, 8 * (part + 1), one_pair, 0)
        columns = pl.ds(1024 * part, 1024)
        into = out_ref.at[pl.ds(2 * k, 2), :, columns]
        mine = pltpu.make_async_copy(
            result.at[:, pl.ds(pl.multiple_of(128 * k, 128), 128), columns], into, out_sem.at[part]
        )
        theirs = pltpu.make_async_remote_copy(
            src_ref=result.at[:, pl.ds(pl.multiple_of(128 - 128 * k, 128), 128), columns], dst_ref=into,
            send_sem=outs_send.at[part], recv_sem=outs_recv.at[part],
            device_id=device(x, y, z, k + 1), device_id_type=MESH,
        )
        theirs.start()
        mine.start()
        finals += [mine, theirs]

    for copy in dy + [c1[slot] for slot in range(1, 16)] + list(c2.values()) + list(c3.values()) + [amp_copy] + sent:
        copy.wait_send()
    for copy in finals:
        copy.wait()


def body(cholesky_c, cholesky_d, amplitudes):
    slab_c = jnp.transpose(cholesky_c, (0, 2, 1)).reshape(2, 20, 16, 1024)
    slab_d = jnp.transpose(cholesky_d, (0, 2, 1)).reshape(2, 20, 16, 1024)
    amps = jnp.transpose(amplitudes.reshape(128, 16, 16), (0, 2, 1)).reshape(128, 256)
    dma = pltpu.SemaphoreType.DMA
    out = pl.pallas_call(
        kernel,
        out_shape=jax.ShapeDtypeStruct((4, 128, 4096), BF16),
        in_specs=[
            pl.BlockSpec(memory_space=pl.ANY),
            pl.BlockSpec(memory_space=pl.ANY),
            pl.BlockSpec(memory_space=pltpu.VMEM),
        ],
        out_specs=pl.BlockSpec(memory_space=pl.ANY),
        scratch_shapes=[
            pltpu.VMEM((20, 16, 1024), BF16),
            pltpu.VMEM((16, 10, 16, 128), BF16),
            pltpu.VMEM((16, 4, 10, 16, 128), BF16),
            pltpu.VMEM((2, 4, 20, 16, 128), BF16),
            pltpu.VMEM((1280, 128), F32),
            pltpu.VMEM((16, 2, 80, 1024), BF16),
            pltpu.VMEM((2, 16, 2, 80, 1024), BF16),
            pltpu.VMEM((1024, 1024), F32),
            pltpu.VMEM((8, 1024, 128), F32),
            pltpu.VMEM((32, 256, 256), BF16),
            pltpu.VMEM((2, 128, 256), BF16),
            pltpu.VMEM((2, 256, 4096), BF16),
            dma((2,)), dma((2,)), dma((16,)), dma((16,)), dma((5, 3)), dma((5, 3)), dma((5,)), dma((5,)),
            dma((3,)), dma((3,)), dma((2, 2, 7)), dma((2, 2, 7)), dma((2, 2, 8)), dma((2, 2, 8)),
            dma((4,)), dma((4,)), dma((4,)),
        ],
        compiler_params=pltpu.CompilerParams(
            collective_id=0, has_side_effects=True, vmem_limit_bytes=56 * 2**20
        ),
        cost_estimate=pl.CostEstimate(flops=13_000_000_000, bytes_accessed=8_000_000, transcendentals=0),
    )(slab_c, slab_d, amps)
    return jnp.transpose(out, (1, 0, 2))


def solution(mesh):
    return jax.shard_map(
        body,
        mesh=mesh,
        in_specs=(P("vir", None, None), P("vir", None, None), P("occ", None)),
        out_specs=P("occ", "vir", None),
        check_vma=False,
    )
```

time: 448 us -> 111 us (0.25)
  waiting for transfers between devices: 230 us -> 0 us
  local copies, waits for them, and re-layouts: 146 us -> 9.15 us
  Pallas kernels: 0 us -> 101 us
  matrix products: 23.2 us -> 0 us
  starting transfers between devices: 22.9 us -> 0 us
  between operations: 13.5 us -> 0.02 us
  other arithmetic: 10.8 us -> 0 us
    all_to_all x2 -> x0, waiting for transfers between devices: 165 us -> none  [the longest x1 97.9 us: body(): lax.all_to_all(send_d, 'vir', split_axis=1, concat_axis=0, tiled=True)]
    pallas_call x0 -> x1, Pallas kernels: none -> 101 us  [body(): pl.pallas_call(kernel, out_shape=jax.ShapeDtypeStruct((4, 128, 4096), BF1...]
    all_gather x1 -> x0, waiting for transfers between devices: 64.9 us -> none  [body(): lax.all_gather(integrals, 'occ', axis=0, tiled=True)]
    another operation x2 -> x0, local copies, waits for them, and re-layouts: 49.9 us -> none
    all_to_all x2 -> x0, local copies, waits for them, and re-layouts: 46.6 us -> none  [the longest x1 23.3 us: body(): lax.all_to_all(send_d, 'vir', split_axis=1, concat_axis=0, tiled=True)]
    dot_general x2 -> x0, matrix products: 23.2 us -> none  [the longest x1 15.5 us: body(): jnp.einsum('qmac,qmbd->mabcd', left_block, right_block, preferred_element...]
    convert_element_type x4 -> x0, local copies, waits for them, and re-layouts: 23.1 us -> none  [the longest x3 15.2 us: body(): summed.reshape(blocks_dev, AH * BH, tile_width * tile_width)]
    all_to_all x2 -> x0, starting transfers between devices: 22.7 us -> none  [the longest x1 13.9 us: body(): lax.all_to_all(send_d, 'vir', split_axis=1, concat_axis=0, tiled=True)]
  transfers between devices with their start and end apart: 3 -> 0, of which waited for: 3 -> 0; matrix products, arithmetic and copies ran while one was open for 15% -> 0% of each run, Pallas kernels for 0% -> 0%
where the time goes in v1:
time: 111 us; the launch traced here: 110 us
  Pallas kernels  101 us (91%)
  local copies, waits for them, and re-layouts  9.15 us (8%)
    pallas_call x1, Pallas kernels, body(): pl.pallas_call(kernel, out_shape=jax.ShapeDtypeStruct((4, 128, 4096), BF1...  101 us
    transpose x1, local copies, waits for them, and re-layouts, body(): return jnp.transpose(out, (1, 0, 2))  7.44 us

profile of v1, /device:TPU:1, one launch (start us, length us, event | category | flops | bytes accessed | tf_op | source)
XLA Modules:
  0.0 110.3 jit_solution(10917941006123396586)
XLA Ops:
  0.0 0.9 copy.6
  1.0 0.7 copy.8.amp_ref
  1.7 101.2 %shard_map.37 = bf16[4,128,4096]{2,1,0:T(8,128)(2,1)} custom-call(bf16[2,20,16,1024]{3,2,1,0:T(8,128)(2,1)} %bitcast.14, bf16[2,20,16,1024]{3,2,1,0:T(8,128)(2,1)} %bitcast.15, bf16[128,256]{1,0:T(8,128)(2,1)} %copy.8.amp_ref), custom_call_target="tpu_custom_call" | custom-call | flops 12999999488 | bytes 8000000 | tf_op jit(solution)/shard_map/pallas_call | solution.py:360
  102.9 7.4 %copy.9 = bf16[128,4,4096]{2,1,0:T(4,128)(2,1)} copy(bf16[128,4,4096]{2,0,1:T(8,128)(2,1)} %bitcast.11) | data formatting | bytes 8388608 | tf_op jit(solution)/shard_map/transpose | solution.py:391
  (1 shorter events, 0.0 us)

commit v2 on v1

v2 whole, which is shorter than its diff:
```python
import functools

import jax
import jax.numpy as jnp
from jax import lax
from jax.experimental import pallas as pl
from jax.experimental.pallas import tpu as pltpu
from jax.sharding import PartitionSpec as P

MESH = pl.DeviceIdType.MESH
F32 = jnp.float32
BF16 = jnp.bfloat16

NX, NY, NZ, NK = 4, 4, 8, 2
OFFSETS = (0, -1, 1, -2, 2, -3, 3, 4)
PARTS = ((0, 0), (0, 1), (1, 0), (1, 1))
ARRIVALS = tuple(
    tuple((sign * hops, h, half) for hops in (1, 2, 3) for h, half in PARTS) + ((4, 0, way), (4, 1, way))
    for way, sign in ((0, -1), (1, 1))
)
SPANS = ((0, 8), (8, 16))
GROUPS = ((0, 2), (2, 4), (6, 4), (10, 4), (14, 2))


def slot_of(offset, other):
    return 2 * OFFSETS.index(offset) + other


def place():
    v, o = lax.axis_index("vir"), lax.axis_index("occ")
    x = (o // NK) * 2 + v // (NZ * NY)
    return x, v % NY, (v // NY) % NZ, o % NK


def device(x, y, z, k):
    x, y, z, k = (x + NX) % NX, (y + NY) % NY, (z + NZ) % NZ, (k + NK) % NK
    return ((x % 2) * NZ + z) * NY + y, (x // 2) * NK + k


def kernel(
    c_ref, d_ref, amp_ref, out_ref,
    c_slab, c_send, c_in, c_raw, d_raw, rows, c_full, d_first, d_second, acc, spread, ints, amps, result,
    load_sem, amp_sems, c1_send, c1_recv, cx_send, cx_recv, c2_send, c2_recv, c3_send, c3_recv, dy_send, dy_recv,
    z_send, z_recv, x_send, x_recv, out_sem, outs_send, outs_recv,
):
    x, y, z, k = place()
    x_low, share = x % 2, 5 * (x // 2)
    d_full = (d_first, d_second)
    low = lax.broadcasted_iota(jnp.int32, (16, 128), 1) < 64

    barrier = pltpu.get_barrier_semaphore()
    greeted = []
    greeted += [device(x, y, z + offset, k) for offset in OFFSETS if offset]
    greeted += [device(x + step, y, z, k) for step in (1, 3)]
    greeted += [device(x, y + step, z, k) for step in (1, 2, 3)]
    greeted.append(device(x, y, z, k + 1))
    for target in greeted:
        pl.semaphore_signal(barrier, inc=1, device_id=target, device_id_type=MESH)

    load = pltpu.make_async_copy(c_ref.at[k], c_slab, load_sem.at[0])
    load.start()
    own_d = pltpu.make_async_copy(
        d_ref.at[:, :, :, pl.ds(pl.multiple_of(256 * y + 128 * k, 128), 128)], d_raw.at[:, y], load_sem.at[1]
    )
    own_d.start()
    pl.semaphore_wait(barrier, len(greeted))

    def columns_of(to, half):
        return d_ref.at[half, :, :, pl.ds(pl.multiple_of(256 * to + 128 * k, 128), 128)]

    dy = {}
    for half in (0, 1):
        for step in (1, 3, 2):
            to = (y + step) % NY
            copy = pltpu.make_async_remote_copy(
                src_ref=columns_of(to, half), dst_ref=d_raw.at[half, y],
                send_sem=dy_send.at[half, step - 1], recv_sem=dy_recv.at[half, step - 1],
                device_id=device(x, to, z, k), device_id_type=MESH,
            )
            copy.start()
            dy[half, step] = copy
    load.wait()

    def pair_up(p, _):
        for m in range(8):
            first = c_slab[2 * p, :, 128 * m : 128 * (m + 1)].astype(F32)
            second = c_slab[2 * p + 1, :, 128 * m : 128 * (m + 1)].astype(F32)
            c_send[m // 4, 2 * m % 8, p] = jnp.where(low, first, pltpu.roll(second, 64, 1)).astype(BF16)
            c_send[m // 4, 2 * m % 8 + 1, p] = jnp.where(low, pltpu.roll(first, 64, 1), second).astype(BF16)
        return 0

    lax.fori_loop(0, 10, pair_up, 0)
    c1, c1_other = {}, {}
    for offset in OFFSETS[1:]:
        to_z = (z - offset + NZ) % NZ
        index = OFFSETS.index(offset)
        for other, copies in ((1, c1_other), (0, c1)):
            copies[offset] = pltpu.make_async_remote_copy(
                src_ref=c_send.at[1 - x_low, to_z, pl.ds(share, 5)] if other else c_send.at[x_low, to_z],
                dst_ref=c_in.at[index] if other else c_raw.at[slot_of(offset, 0), y],
                send_sem=c1_send.at[other, index], recv_sem=c1_recv.at[other, index],
                device_id=device(x, y, to_z, k), device_id_type=MESH,
            )
            copies[offset].start()
    own_c = pltpu.make_async_copy(c_send.at[x_low, z], c_raw.at[0, y], load_sem.at[0])
    own_c.start()

    old, new = (lax.broadcasted_iota(jnp.int32, (256, 256), axis) for axis in (0, 1))
    swap = (old == (new % 16) * 16 + new // 16).astype(F32).astype(BF16)
    amps[k] = jnp.dot(amp_ref[...], swap, preferred_element_type=F32).astype(BF16)
    amp_copy = pltpu.make_async_remote_copy(
        src_ref=amps.at[k], dst_ref=amps.at[k], send_sem=amp_sems.at[0], recv_sem=amp_sems.at[1],
        device_id=device(x, y, z, k + 1), device_id_type=MESH,
    )
    amp_copy.start()

    cx = {}

    def c_across(offset):
        index = OFFSETS.index(offset)
        if offset:
            c1_other[offset].wait_recv()
        for step in (1, 3):
            cx[offset, step] = pltpu.make_async_remote_copy(
                src_ref=c_in.at[index] if offset else c_send.at[1 - x_low, z, pl.ds(share, 5)],
                dst_ref=c_raw.at[slot_of(offset, 1), y, pl.ds(share, 5)],
                send_sem=cx_send.at[index, step // 2], recv_sem=cx_recv.at[index, step // 2],
                device_id=device(x + step, y, z, k), device_id_type=MESH,
            )
            cx[offset, step].start()

    c2 = {}

    def c_forward(group):
        start, count = GROUPS[group]
        for offset in OFFSETS[start // 2 : (start + count) // 2]:
            if offset:
                c1[offset].wait_recv()
            else:
                own_c.wait()
            for step in (1, 3):
                cx[offset, step].wait_recv()
        mine = c_raw.at[pl.ds(start, count), y]
        for step in (1, 3, 2):
            copy = pltpu.make_async_remote_copy(
                src_ref=mine, dst_ref=mine,
                send_sem=c2_send.at[group, step - 1], recv_sem=c2_recv.at[group, step - 1],
                device_id=device(x, y + step, z, k), device_id_type=MESH,
            )
            copy.start()
            c2[group, step] = copy

    c3 = {}

    def c_rows(group):
        start, count = GROUPS[group]
        for step in (1, 2, 3):
            c2[group, step].wait_recv()

        def one_slot(slot, _):
            rows[0:640, :] = c_raw[slot].reshape(640, 128).astype(F32)
            lower = lax.broadcasted_iota(jnp.int32, (40, 128), 1) < 64
            for m in range(8):
                first = rows[pl.ds(2 * m, 40, stride=16), :]
                second = rows[pl.ds(2 * m + 1, 40, stride=16), :]
                both = jnp.concatenate(
                    [
                        jnp.where(lower, first, pltpu.roll(second, 64, 1)),
                        jnp.where(lower, pltpu.roll(first, 64, 1), second),
                    ],
                    axis=0,
                )
                c_full[slot, k, :, 128 * m : 128 * (m + 1)] = both.astype(BF16)
            return 0

        lax.fori_loop(start, start + count, one_slot, 0)
        half = c_full.at[pl.ds(start, count), k]
        c3[group] = pltpu.make_async_remote_copy(
            src_ref=half, dst_ref=half, send_sem=c3_send.at[group], recv_sem=c3_recv.at[group],
            device_id=device(x, y, z, k + 1), device_id_type=MESH,
        )
        c3[group].start()

    sent = []

    def x_copy(h, offset, half):
        copy = pltpu.make_async_remote_copy(
            src_ref=d_full[h].at[slot_of(offset, 0), half],
            dst_ref=d_full[h].at[slot_of(offset, 1), half],
            send_sem=x_send.at[h, half, OFFSETS.index(offset)],
            recv_sem=x_recv.at[h, half, OFFSETS.index(offset)],
            device_id=device(x + 1 - 2 * (half if offset else h), y, z, k), device_id_type=MESH,
        )
        return copy

    def x_start(h, offset, half):
        copy = x_copy(h, offset, half)
        copy.start()
        sent.append(copy)

    def z_copy(way, i):
        offset, h, half = ARRIVALS[way][i]
        before = (offset + 1 if way == 0 else offset - 1) if offset != 4 else (-3 if way == 0 else 3)
        return pltpu.make_async_remote_copy(
            src_ref=d_full[h].at[slot_of(before, 0), half],
            dst_ref=d_full[h].at[slot_of(offset, 0), half],
            send_sem=z_send.at[way, i], recv_sem=z_recv.at[way, i],
            device_id=device(x, y, z + 1 - 2 * way, k), device_id_type=MESH,
        )

    def z_start(way, i):
        copy = z_copy(way, i)
        copy.start()
        sent.append(copy)

    def own_start(h, half):
        for way in (0, 1):
            z_start(way, PARTS.index((h, half)))

    def step(i):
        for way in (0, 1):
            z_copy(way, i).wait_recv()
            offset, h, half = ARRIVALS[way][i]
            after = offset - 1 if way == 0 else offset + 1
            onward = (4 if after == -4 else after, h, half)
            if onward in ARRIVALS[way]:
                z_start(way, ARRIVALS[way].index(onward))
            x_start(h, offset, half)

    def await_x(h, group):
        start, count = GROUPS[group]
        for slot in range(start, start + count, 2):
            for half in (0, 1):
                x_copy(h, OFFSETS[slot // 2], half).wait_recv()

    def multiply(h, group):
        start, count = GROUPS[group]
        last = group == len(GROUPS) - 1
        values = SPANS[h][1] - SPANS[h][0]

        def one_tile(m, _):
            columns = pl.ds(pl.multiple_of(256 * m, 256), 256)
            left = c_full[start : start + count, :, :, columns].reshape(160 * count, 256)
            right = d_full[h][start : start + count].reshape(160 * count, 128 * values)
            term = lax.dot_general(left, right, (((0,), (0,)), ((), ())), preferred_element_type=F32)
            if group:
                term += acc[columns, 128 * SPANS[h][0] : 128 * SPANS[h][1]]
            if not last:
                acc[columns, 128 * SPANS[h][0] : 128 * SPANS[h][1]] = term
            else:
                for c in range(4):
                    for d in range(values):
                        spread[d, pl.ds(4 * m + c, 64, stride=16), :] = term[
                            64 * c : 64 * (c + 1), 128 * d : 128 * (d + 1)
                        ]
            return 0

        lax.fori_loop(0, 4, one_tile, 0, unroll=4 if last else 2)

    def term(h, group):
        if not h:
            c3[group].wait_recv()
        await_x(h, group)
        multiply(h, group)

    def round_off(h):
        start, stop = SPANS[h]

        def one_pair(pair, _):
            for d in range(start, stop):
                first = spread[d - start, pl.ds(pl.multiple_of(32 * pair, 16), 16), :]
                second = spread[d - start, pl.ds(pl.multiple_of(32 * pair + 16, 16), 16), :]
                at = slice(16 * d, 16 * (d + 1))
                ints[pair, at, 0:128] = jnp.where(low, first, pltpu.roll(second, 64, 1)).astype(BF16)
                ints[pair, at, 128:256] = jnp.where(low, pltpu.roll(first, 64, 1), second).astype(BF16)
            return 0

        lax.fori_loop(0, 32, one_pair, 0, unroll=8)

    c_across(0)

    def d_rows(half):
        rows[...] = d_raw[half].reshape(1280, 128).astype(F32)
        for h, (start, stop) in enumerate(SPANS):
            for d in range(start, stop):
                both = jnp.concatenate([rows[pl.ds(16 * odd + d, 40, stride=32), :] for odd in (0, 1)], axis=0)
                d_full[h][0, half, :, 128 * (d - start) : 128 * (d - start + 1)] = both.astype(BF16)

    own_d.wait()
    for half in (0, 1):
        for step_y in (1, 3, 2):
            dy[half, step_y].wait_recv()
        d_rows(half)
        own_start(0, half)
        x_start(0, 0, half)
        x_start(1, 0, half)
    own_start(1, 0)
    own_start(1, 1)
    for offset in OFFSETS[1:]:
        c_across(offset)
    c_forward(0)
    c_forward(1)
    step(0)
    c_forward(2)
    step(1)
    c_forward(3)
    c_forward(4)
    c_rows(0)
    step(2)
    step(3)
    c_rows(1)
    term(0, 0)
    step(4)
    term(1, 0)
    step(5)
    c_rows(2)
    term(0, 1)
    step(6)
    term(1, 1)
    step(7)
    step(8)
    c_rows(3)
    term(0, 2)
    step(9)
    c_rows(4)
    term(1, 2)
    step(10)
    step(11)
    step(12)
    term(0, 3)
    step(13)
    term(1, 3)
    amp_copy.wait_recv()
    term(0, 4)
    round_off(0)
    term(1, 4)
    round_off(1)

    finals = []
    for part in range(4):

        def one_pair(pair, _):
            total = jnp.dot(amps[...].reshape(256, 256), ints[pair], preferred_element_type=F32)
            columns = pl.ds(pl.multiple_of(128 * pair, 128), 128)
            result[0, :, columns] = total[:, :128].astype(BF16)
            result[1, :, columns] = total[:, 128:].astype(BF16)
            return 0

        lax.fori_loop(8 * part, 8 * (part + 1), one_pair, 0, unroll=8)
        columns = pl.ds(1024 * part, 1024)
        into = out_ref.at[pl.ds(2 * k, 2), :, columns]
        mine = pltpu.make_async_copy(
            result.at[:, pl.ds(pl.multiple_of(128 * k, 128), 128), columns], into, out_sem.at[part]
        )
        theirs = pltpu.make_async_remote_copy(
            src_ref=result.at[:, pl.ds(pl.multiple_of(128 - 128 * k, 128), 128), columns], dst_ref=into,
            send_sem=outs_send.at[part], recv_sem=outs_recv.at[part],
            device_id=device(x, y, z, k + 1), device_id_type=MESH,
        )
        theirs.start()
        mine.start()
        finals += [mine, theirs]

    for copy in list(dy.values()) + list(c1.values()) + list(c1_other.values()) + list(cx.values()) + list(c2.values()) + list(c3.values()) + [amp_copy] + sent:
        copy.wait_send()
    for copy in finals:
        copy.wait()


def blocks_inward(in_ref, out_ref):
    out_ref[...] = jnp.swapaxes(in_ref[...], 0, 1)


def body(cholesky_c, cholesky_d, amplitudes):
    slab_c = jnp.transpose(cholesky_c, (0, 2, 1)).reshape(2, 20, 16, 1024)
    slab_d = jnp.transpose(cholesky_d, (0, 2, 1)).reshape(2, 20, 16, 1024)
    dma = pltpu.SemaphoreType.DMA
    out = pl.pallas_call(
        kernel,
        out_shape=jax.ShapeDtypeStruct((4, 128, 4096), BF16),
        in_specs=[
            pl.BlockSpec(memory_space=pl.ANY),
            pl.BlockSpec(memory_space=pl.ANY),
            pl.BlockSpec(memory_space=pltpu.VMEM),
        ],
        out_specs=pl.BlockSpec(memory_space=pl.ANY),
        scratch_shapes=[
            pltpu.VMEM((20, 16, 1024), BF16),
            pltpu.VMEM((2, 8, 10, 16, 128), BF16),
            pltpu.VMEM((8, 5, 16, 128), BF16),
            pltpu.VMEM((16, 4, 10, 16, 128), BF16),
            pltpu.VMEM((2, 4, 20, 16, 128), BF16),
            pltpu.VMEM((1280, 128), F32),
            pltpu.VMEM((16, 2, 80, 1024), BF16),
            *(pltpu.VMEM((16, 2, 80, 128 * (stop - start)), BF16) for start, stop in SPANS),
            pltpu.VMEM((1024, 2048), F32),
            pltpu.VMEM((SPANS[0][1], 1024, 128), F32),
            pltpu.VMEM((32, 256, 256), BF16),
            pltpu.VMEM((2, 128, 256), BF16),
            pltpu.VMEM((2, 256, 4096), BF16),
            dma((2,)), dma((2,)), dma((2, 8)), dma((2, 8)), dma((8, 2)), dma((8, 2)), dma((5, 3)), dma((5, 3)), dma((5,)), dma((5,)),
            dma((2, 3)), dma((2, 3)), dma((2, 14)), dma((2, 14)), dma((2, 2, 8)), dma((2, 2, 8)),
            dma((4,)), dma((4,)), dma((4,)),
        ],
        compiler_params=pltpu.CompilerParams(
            collective_id=0, has_side_effects=True, vmem_limit_bytes=63 * 2**20
        ),
        cost_estimate=pl.CostEstimate(flops=13_000_000_000, bytes_accessed=8_000_000, transcendentals=0),
    )(slab_c, slab_d, amplitudes)
    return pl.pallas_call(
        blocks_inward,
        grid=(2,),
        out_shape=jax.ShapeDtypeStruct((128, 4, 4096), BF16),
        in_specs=[pl.BlockSpec((4, 128, 2048), lambda i: (0, 0, i))],
        out_specs=pl.BlockSpec((128, 4, 2048), lambda i: (0, 0, i)),
        compiler_params=pltpu.CompilerParams(vmem_limit_bytes=56 * 2**20),
    )(out)


def solution(mesh):
    return jax.shard_map(
        body,
        mesh=mesh,
        in_specs=(P("vir", None, None), P("vir", None, None), P("occ", None)),
        out_specs=P("occ", "vir", None),
        check_vma=False,
    )
```

time: 111 us -> 97.2 us (0.88)
  local copies, waits for them, and re-layouts: 9.15 us -> 0 us
  Pallas kernels: 101 us -> 97.1 us
    pallas_call x1, Pallas kernels: 101 us -> 93.1 us  [body(): pl.pallas_call(kernel, out_shape=jax.ShapeDtypeStruct((4, 128, 4096), BF1...]
    transpose x2 -> x0, local copies, waits for them, and re-layouts: 7.46 us -> none  [the longest x1 7.44 us: body(): return jnp.transpose(out, (1, 0, 2))]
    pallas_call x0 -> x1, Pallas kernels: none -> 3.97 us  [body(): pl.pallas_call(blocks_inward, grid=(2,), out_shape=jax.ShapeDtypeStruct((...]
where the time goes in v2:
time: 97.2 us; the launch traced here: 97.1 us
  Pallas kernels  97.1 us (100%)
    pallas_call x1, Pallas kernels, body(): pl.pallas_call(kernel, out_shape=jax.ShapeDtypeStruct((4, 128, 4096), BF1...  93.1 us
    pallas_call x1, Pallas kernels, body(): pl.pallas_call(blocks_inward, grid=(2,), out_shape=jax.ShapeDtypeStruct((...  3.97 us

profile of v2, /device:TPU:1, one launch (start us, length us, event | category | flops | bytes accessed | tf_op | source)
XLA Modules:
  0.0 97.1 jit_solution(14999145742361379468)
XLA Ops:
  0.0 93.1 %shard_map.37.in_ref = bf16[4,128,4096]{2,1,0:T(8,128)(2,1)} custom-call(bf16[2,20,16,1024]{3,2,1,0:T(8,128)(2,1)} %bitcast.6, bf16[2,20,16,1024]{3,2,1,0:T(8,128)(2,1)} %bitcast.7, bf16[128,256]{1,0:T(8,128)(2,1)} %amp_ref.1), custom_call_target="tpu_custom_call" | custom-call | flops 12999999488 | bytes 8000000 | tf_op jit(solution)/shard_map/pallas_call | solution.py:378
  93.1 4.0 %shard_map.38 = bf16[128,4,4096]{2,1,0:T(4,128)(2,1)} custom-call(bf16[4,128,4096]{2,1,0:T(8,128)(2,1)} %shard_map.37.in_ref), custom_call_target="tpu_custom_call" | custom-call | tf_op jit(solution)/shard_map/pallas_call | solution.py:410

commit v3 on v2

--- a/solution.py
+++ b/solution.py
@@ -41,7 +41,7 @@
     c_ref, d_ref, amp_ref, out_ref,
     c_slab, c_send, c_in, c_raw, d_raw, rows, c_full, d_first, d_second, acc, spread, ints, amps, result,
     load_sem, amp_sems, c1_send, c1_recv, cx_send, cx_recv, c2_send, c2_recv, c3_send, c3_recv, dy_send, dy_recv,
-    z_send, z_recv, x_send, x_recv, out_sem, outs_send, outs_recv,
+    z_send, z_recv, x_send, x_recv, outs_send, outs_recv,
 ):
     x, y, z, k = place()
     x_low, share = x % 2, 5 * (x // 2)
@@ -107,9 +107,9 @@
 
     old, new = (lax.broadcasted_iota(jnp.int32, (256, 256), axis) for axis in (0, 1))
     swap = (old == (new % 16) * 16 + new // 16).astype(F32).astype(BF16)
-    amps[k] = jnp.dot(amp_ref[...], swap, preferred_element_type=F32).astype(BF16)
+    amps[0] = jnp.dot(amp_ref[...], swap, preferred_element_type=F32).astype(BF16)
     amp_copy = pltpu.make_async_remote_copy(
-        src_ref=amps.at[k], dst_ref=amps.at[k], send_sem=amp_sems.at[0], recv_sem=amp_sems.at[1],
+        src_ref=amps.at[0], dst_ref=amps.at[1], send_sem=amp_sems.at[0], recv_sem=amp_sems.at[1],
         device_id=device(x, y, z, k + 1), device_id_type=MESH,
     )
     amp_copy.start()
@@ -342,24 +342,21 @@
         def one_pair(pair, _):
             total = jnp.dot(amps[...].reshape(256, 256), ints[pair], preferred_element_type=F32)
             columns = pl.ds(pl.multiple_of(128 * pair, 128), 128)
-            result[0, :, columns] = total[:, :128].astype(BF16)
-            result[1, :, columns] = total[:, 128:].astype(BF16)
+            for j in (0, 1):
+                rounded = total[:, 128 * j : 128 * (j + 1)].astype(BF16)
+                out_ref[2 * k + j, :, columns] = rounded[:128]
+                result[j, :, columns] = rounded[128:]
             return 0
 
         lax.fori_loop(8 * part, 8 * (part + 1), one_pair, 0, unroll=8)
         columns = pl.ds(1024 * part, 1024)
-        into = out_ref.at[pl.ds(2 * k, 2), :, columns]
-        mine = pltpu.make_async_copy(
-            result.at[:, pl.ds(pl.multiple_of(128 * k, 128), 128), columns], into, out_sem.at[part]
-        )
         theirs = pltpu.make_async_remote_copy(
-            src_ref=result.at[:, pl.ds(pl.multiple_of(128 - 128 * k, 128), 128), columns], dst_ref=into,
+            src_ref=result.at[:, :, columns], dst_ref=out_ref.at[pl.ds(2 * k, 2), :, columns],
             send_sem=outs_send.at[part], recv_sem=outs_recv.at[part],
             device_id=device(x, y, z, k + 1), device_id_type=MESH,
         )
         theirs.start()
-        mine.start()
-        finals += [mine, theirs]
+        finals.append(theirs)
 
     for copy in list(dy.values()) + list(c1.values()) + list(c1_other.values()) + list(cx.values()) + list(c2.values()) + list(c3.values()) + [amp_copy] + sent:
         copy.wait_send()
@@ -368,7 +365,8 @@
 
 
 def blocks_inward(in_ref, out_ref):
-    out_ref[...] = jnp.swapaxes(in_ref[...], 0, 1)
+    columns = pl.ds(pl.multiple_of(1024 * pl.program_id(0), 1024), 1024)
+    out_ref[...] = jnp.swapaxes(in_ref[:, :, columns], 0, 1)
 
 
 def body(cholesky_c, cholesky_d, amplitudes):
@@ -377,13 +375,13 @@
     dma = pltpu.SemaphoreType.DMA
     out = pl.pallas_call(
         kernel,
-        out_shape=jax.ShapeDtypeStruct((4, 128, 4096), BF16),
+        out_shape=pltpu.VMEM((4, 128, 4096), BF16),
         in_specs=[
             pl.BlockSpec(memory_space=pl.ANY),
             pl.BlockSpec(memory_space=pl.ANY),
             pl.BlockSpec(memory_space=pltpu.VMEM),
         ],
-        out_specs=pl.BlockSpec(memory_space=pl.ANY),
+        out_specs=pl.BlockSpec(memory_space=pltpu.VMEM),
         scratch_shapes=[
             pltpu.VMEM((20, 16, 1024), BF16),
             pltpu.VMEM((2, 8, 10, 16, 128), BF16),
@@ -397,23 +395,23 @@
             pltpu.VMEM((SPANS[0][1], 1024, 128), F32),
             pltpu.VMEM((32, 256, 256), BF16),
             pltpu.VMEM((2, 128, 256), BF16),
-            pltpu.VMEM((2, 256, 4096), BF16),
+            pltpu.VMEM((2, 128, 4096), BF16),
             dma((2,)), dma((2,)), dma((2, 8)), dma((2, 8)), dma((8, 2)), dma((8, 2)), dma((5, 3)), dma((5, 3)), dma((5,)), dma((5,)),
             dma((2, 3)), dma((2, 3)), dma((2, 14)), dma((2, 14)), dma((2, 2, 8)), dma((2, 2, 8)),
-            dma((4,)), dma((4,)), dma((4,)),
+            dma((4,)), dma((4,)),
         ],
         compiler_params=pltpu.CompilerParams(
-            collective_id=0, has_side_effects=True, vmem_limit_bytes=63 * 2**20
+            collective_id=0, has_side_effects=True, vmem_limit_bytes=58 * 2**20
         ),
         cost_estimate=pl.CostEstimate(flops=13_000_000_000, bytes_accessed=8_000_000, transcendentals=0),
     )(slab_c, slab_d, amplitudes)
     return pl.pallas_call(
         blocks_inward,
-        grid=(2,),
+        grid=(4,),
         out_shape=jax.ShapeDtypeStruct((128, 4, 4096), BF16),
-        in_specs=[pl.BlockSpec((4, 128, 2048), lambda i: (0, 0, i))],
-        out_specs=pl.BlockSpec((128, 4, 2048), lambda i: (0, 0, i)),
-        compiler_params=pltpu.CompilerParams(vmem_limit_bytes=56 * 2**20),
+        in_specs=[pl.BlockSpec(memory_space=pltpu.VMEM)],
+        out_specs=pl.BlockSpec((128, 4, 1024), lambda i: (0, 0, i)),
+        compiler_params=pltpu.CompilerParams(vmem_limit_bytes=24 * 2**20),
     )(out)
 
 

time: 97.2 us -> 95.7 us (0.985)
  Pallas kernels: 97.1 us -> 95.6 us
    pallas_call x2, Pallas kernels: 97.1 us -> 95.6 us  [the longest x1 92.9 us: body(): pl.pallas_call(kernel, out_shape=pltpu.VMEM((4, 128, 4096), BF16), in_spe...]
where the time goes in v3:
time: 95.7 us; the launch traced here: 95.6 us
  Pallas kernels  95.6 us (100%)
    pallas_call x1, Pallas kernels, body(): pl.pallas_call(kernel, out_shape=pltpu.VMEM((4, 128, 4096), BF16), in_spe...  92.9 us
    pallas_call x1, Pallas kernels, body(): pl.pallas_call(blocks_inward, grid=(4,), out_shape=jax.ShapeDtypeStruct((...  2.67 us

profile of v3, /device:TPU:1, one launch (start us, length us, event | category | flops | bytes accessed | tf_op | source)
XLA Modules:
  0.0 95.6 jit_solution(5357775431021232803)
XLA Ops:
  0.0 92.9 %shard_map.37.in_ref = bf16[4,128,4096]{2,1,0:T(8,128)(2,1)S(1)} custom-call(bf16[2,20,16,1024]{3,2,1,0:T(8,128)(2,1)} %bitcast.6, bf16[2,20,16,1024]{3,2,1,0:T(8,128)(2,1)} %bitcast.7, bf16[128,256]{1,0:T(8,128)(2,1)} %amp_ref.1), custom_call_target="tpu_custom_call" | custom-call | flops 12999999488 | bytes 8000000 | tf_op jit(solution)/shard_map/pallas_call | solution.py:376
  92.9 2.7 %shard_map.38 = bf16[128,4,4096]{2,1,0:T(4,128)(2,1)} custom-call(bf16[4,128,4096]{2,1,0:T(8,128)(2,1)S(1)} %shard_map.37.in_ref), custom_call_target="tpu_custom_call" | custom-call | tf_op jit(solution)/shard_map/pallas_call | solution.py:408

commit v4 on v3

--- a/solution.py
+++ b/solution.py
@@ -255,7 +255,7 @@
                         ]
             return 0
 
-        lax.fori_loop(0, 4, one_tile, 0, unroll=4 if last else 2)
+        lax.fori_loop(0, 4, one_tile, 0, unroll=4)
 
     def term(h, group):
         if not h:
@@ -325,11 +325,16 @@
     c_rows(4)
     term(1, 2)
     step(10)
+    for copy in [*dy.values(), *c1.values(), *c1_other.values(), *cx.values(), *c2.values(), *c3.values()]:
+        copy.wait_send()
     step(11)
     step(12)
     term(0, 3)
     step(13)
     term(1, 3)
+    settled = sent[:40]
+    for copy in settled:
+        copy.wait_send()
     amp_copy.wait_recv()
     term(0, 4)
     round_off(0)
@@ -358,7 +363,7 @@
         theirs.start()
         finals.append(theirs)
 
-    for copy in list(dy.values()) + list(c1.values()) + list(c1_other.values()) + list(cx.values()) + list(c2.values()) + list(c3.values()) + [amp_copy] + sent:
+    for copy in [amp_copy] + sent[len(settled) :]:
         copy.wait_send()
     for copy in finals:
         copy.wait()
@@ -401,7 +406,7 @@
             dma((4,)), dma((4,)),
         ],
         compiler_params=pltpu.CompilerParams(
-            collective_id=0, has_side_effects=True, vmem_limit_bytes=58 * 2**20
+            collective_id=0, has_side_effects=True, vmem_limit_bytes=59 * 2**20
         ),
         cost_estimate=pl.CostEstimate(flops=13_000_000_000, bytes_accessed=8_000_000, transcendentals=0),
     )(slab_c, slab_d, amplitudes)

time: 95.7 us -> 96.1 us (level)
  no operation moved by 1% of the time
where the time goes in v4:
time: 96.1 us; the launch traced here: 96 us
  Pallas kernels  96 us (100%)
    pallas_call x1, Pallas kernels, body(): pl.pallas_call(kernel, out_shape=pltpu.VMEM((4, 128, 4096), BF16), in_spe...  93.3 us
    pallas_call x1, Pallas kernels, body(): pl.pallas_call(blocks_inward, grid=(4,), out_shape=jax.ShapeDtypeStruct((...  2.67 us

profile of v4, /device:TPU:1, one launch (start us, length us, event | category | flops | bytes accessed | tf_op | source)
XLA Modules:
  0.0 96.0 jit_solution(2863461728339751680)
XLA Ops:
  0.0 93.3 %shard_map.37.in_ref = bf16[4,128,4096]{2,1,0:T(8,128)(2,1)S(1)} custom-call(bf16[2,20,16,1024]{3,2,1,0:T(8,128)(2,1)} %bitcast.6, bf16[2,20,16,1024]{3,2,1,0:T(8,128)(2,1)} %bitcast.7, bf16[128,256]{1,0:T(8,128)(2,1)} %amp_ref.1), custom_call_target="tpu_custom_call" | custom-call | flops 12999999488 | bytes 8000000 | tf_op jit(solution)/shard_map/pallas_call | solution.py:381
  93.3 2.7 %shard_map.38 = bf16[128,4,4096]{2,1,0:T(4,128)(2,1)} custom-call(bf16[4,128,4096]{2,1,0:T(8,128)(2,1)S(1)} %shard_map.37.in_ref), custom_call_target="tpu_custom_call" | custom-call | tf_op jit(solution)/shard_map/pallas_call | solution.py:413

commit v5 on v3

--- a/solution.py
+++ b/solution.py
@@ -280,7 +280,7 @@
     c_across(0)
 
     def d_rows(half):
-        rows[...] = d_raw[half].reshape(1280, 128).astype(F32)
+        rows[0:1280, :] = d_raw[half].reshape(1280, 128).astype(F32)
         for h, (start, stop) in enumerate(SPANS):
             for d in range(start, stop):
                 both = jnp.concatenate([rows[pl.ds(16 * odd + d, 40, stride=32), :] for odd in (0, 1)], axis=0)
@@ -388,11 +388,11 @@
             pltpu.VMEM((8, 5, 16, 128), BF16),
             pltpu.VMEM((16, 4, 10, 16, 128), BF16),
             pltpu.VMEM((2, 4, 20, 16, 128), BF16),
-            pltpu.VMEM((1280, 128), F32),
+            pltpu.VMEM((1312, 128), F32),
             pltpu.VMEM((16, 2, 80, 1024), BF16),
             *(pltpu.VMEM((16, 2, 80, 128 * (stop - start)), BF16) for start, stop in SPANS),
             pltpu.VMEM((1024, 2048), F32),
-            pltpu.VMEM((SPANS[0][1], 1024, 128), F32),
+            pltpu.VMEM((SPANS[0][1], 1040, 128), F32),
             pltpu.VMEM((32, 256, 256), BF16),
             pltpu.VMEM((2, 128, 256), BF16),
             pltpu.VMEM((2, 128, 4096), BF16),

time: 95.7 us -> 95.7 us (level)
  no operation moved by 1% of the time
where the time goes in v5:
time: 95.7 us; the launch traced here: 95.6 us
  Pallas kernels  95.6 us (100%)
    pallas_call x1, Pallas kernels, body(): pl.pallas_call(kernel, out_shape=pltpu.VMEM((4, 128, 4096), BF16), in_spe...  92.9 us
    pallas_call x1, Pallas kernels, body(): pl.pallas_call(blocks_inward, grid=(4,), out_shape=jax.ShapeDtypeStruct((...  2.67 us

profile of v5, /device:TPU:1, one launch (start us, length us, event | category | flops | bytes accessed | tf_op | source)
XLA Modules:
  0.0 95.6 jit_solution(4209840779127913878)
XLA Ops:
  0.0 92.9 %shard_map.37.in_ref = bf16[4,128,4096]{2,1,0:T(8,128)(2,1)S(1)} custom-call(bf16[2,20,16,1024]{3,2,1,0:T(8,128)(2,1)} %bitcast.6, bf16[2,20,16,1024]{3,2,1,0:T(8,128)(2,1)} %bitcast.7, bf16[128,256]{1,0:T(8,128)(2,1)} %amp_ref.1), custom_call_target="tpu_custom_call" | custom-call | flops 12999999488 | bytes 8000000 | tf_op jit(solution)/shard_map/pallas_call | solution.py:376
  92.9 2.7 %shard_map.38 = bf16[128,4,4096]{2,1,0:T(4,128)(2,1)} custom-call(bf16[4,128,4096]{2,1,0:T(8,128)(2,1)S(1)} %shard_map.37.in_ref), custom_call_target="tpu_custom_call" | custom-call | tf_op jit(solution)/shard_map/pallas_call | solution.py:408
